TPU v7x, 32 devices: a whole 2x2x4 slice. The times are simulated.
32 devices in a mesh: mem: 16 (over z, y, x), camp: 2 (over core).
Axes of the slice: x: 2, y: 2, z: 4, core: 2. Of those that a mesh axis runs over, the one named last changes fastest.
Arguments:
- gains: bfloat16 [640, 128, 256], P('mem', None, 'camp'), may hold values from -14 to 14
- costs: bfloat16 [640, 128, 256], P('mem', None, 'camp'), may hold values from 0.5 to 2
- tile_rows: int32 [640, 2], P('mem', 'camp'), may hold values from 0 to 7, as said below
- tile_cols: int32 [640, 2], P('mem', 'camp'), may hold values from 0 to 1023
- tile_count: int32 [16, 2], P('mem', 'camp'), may hold values from 1 to 40, as said below
- duals: float32 [262144], P('camp'), may hold values from 0.005 to 0.04
- allowances: float32 [262144], P('camp'), may hold values from 0.02 to 0.16
Outputs:
- duals_out: float32 [262144], P('camp')
- usage_out: float32 [262144], P('camp')
- unused_share: float32 [16384], P('mem')
Inputs may be any that keep to these rules, and one draw needn't show every extreme that they name: `tile_rows`: the live slots of one device name distinct pairs of member block and campaign block. `tile_count`: some device has all 40 slots live.
All inputs are finite; a program needn't handle non-finite values.
Results may differ from a plain program's by a relative error of at most 0.0003.
Values sent between devices are 32-bit elements; how exact they have to be, the bound alone decides.
A program may use at most 64 MiB of HBM per device.

v0:
```python
import jax
import jax.numpy as jnp
from jax import lax
from jax.sharding import PartitionSpec as P

MB = 8
ROUNDS = 3


SMOOTHING = 0.05
STEP_SIZE = 0.2


def local(gains, costs, tile_rows, tile_cols, tile_count, duals, allowances):
    slots = gains.shape[0]
    tile = gains.shape[1]
    camp_blocks = duals.shape[0] // tile
    live_slot = jnp.arange(slots) < tile_count[0, 0]
    member_block = tile_rows[:, 0]
    camp_block = tile_cols[:, 0]
    onehot = (member_block[None, :] == jnp.arange(MB)[:, None]) & live_slot[None, :]
    onehot_f = onehot.astype(jnp.float32)
    gain_f = gains.astype(jnp.float32)
    cost_f = costs.astype(jnp.float32)
    price = duals
    usage = jnp.zeros_like(duals)
    row_top = jnp.zeros((MB, tile), jnp.float32)
    denom = jnp.ones((MB, tile), jnp.float32)
    for step in range(ROUNDS):
        price_tile = jnp.take(price.reshape(camp_blocks, tile), camp_block, axis=0)
        scores = (gain_f - cost_f * price_tile[:, None, :]) / SMOOTHING
        tile_top = jnp.max(scores, axis=2)
        local_top = jnp.maximum(
            jnp.max(jnp.where(onehot[:, :, None], tile_top[None], -jnp.inf), axis=1), 0.0
        )
        row_top = lax.pmax(local_top, "camp")
        exponent = jnp.exp(scores - jnp.take(row_top, member_block, axis=0)[:, :, None])
        tile_sum = jnp.where(live_slot[:, None], jnp.sum(exponent, axis=2), 0.0)
        local_sum = jnp.dot(onehot_f, tile_sum, precision=lax.Precision.HIGHEST)
        row_sum = lax.psum(local_sum, "camp")
        denom = jnp.exp(-row_top) + row_sum
        alloc = exponent / jnp.take(denom, member_block, axis=0)[:, :, None]
        column_use = jnp.where(live_slot[:, None], jnp.sum(cost_f * alloc, axis=1), 0.0)
        local_use = jax.ops.segment_sum(column_use, camp_block, num_segments=camp_blocks).reshape(
            -1
        )
        usage = lax.psum(local_use, "mem")
        price = jnp.maximum(price + STEP_SIZE * (usage - allowances), 0.0)
    unused_share = (jnp.exp(-row_top) / denom).reshape(-1)
    return (price, usage, unused_share)


def solution(mesh):
    return jax.shard_map(
        local,
        mesh=mesh,
        in_specs=(
            P("mem", None, "camp"),
            P("mem", None, "camp"),
            P("mem", "camp"),
            P("mem", "camp"),
            P("mem", "camp"),
            P("camp"),
            P("camp"),
        ),
        out_specs=(P("camp"), P("camp"), P("mem")),
        check_vma=False,
    )
```

profile of v0, /device:TPU:0, one launch (start us, length us, event | category | flops | bytes accessed | tf_op | source)
XLA Modules:
  0.0 396.6 jit_solution(7844415884856842287)
XLA Ops:
  7.2 0.7 compare_and_fusion
  8.5 0.7 compare_and_fusion.1
  9.2 0.7 compare_select_fusion.1
  10.5 0.7 fusion.40
  11.2 1.6 gather_fusion
  12.9 2.6 fusion.7
  15.7 2.6 pmax.21
  18.9 1.7 fusion.6
  20.8 2.5 psum.42
  24.0 1.8 fusion.3
  25.8 1.7 scatter_custom_fusion
  27.6 111.0 %all-reduce.4.cloned.1.call-done = f32[131072]{0:T(1024)} async-done(((f32[131072]{0:T(1024)}), f32[131072]{0:T(1024)}) %all-reduce.4.cloned.1.call-update) | async-done | bytes 524304 | tf_op jit(solution)/shard_map/psum | solution.py:47
  138.5 2.1 fusion.18
  140.6 1.6 gather_fusion.3
  142.3 0.8 fusion.9
  143.2 2.5 pmax.22
  146.3 1.7 fusion.8
  148.2 2.5 psum.44
  151.3 1.8 fusion.4
  153.1 1.7 scatter_custom_fusion.1
  154.9 107.4 %all-reduce.6.cloned.1.call-done = f32[131072]{0:T(1024)} async-done(((f32[131072]{0:T(1024)}), f32[131072]{0:T(1024)}) %all-reduce.6.cloned.1.call-update) | async-done | bytes 524304 | tf_op jit(solution)/shard_map/psum | solution.py:47
  262.3 2.3 fusion.48
  264.6 1.6 gather_fusion.6
  266.3 0.8 fusion.11
  267.2 2.5 pmax.23
  270.3 1.7 fusion.10
  272.2 2.5 psum.46
  275.9 1.8 fusion.5
  277.7 1.8 scatter_custom_fusion.2
  279.6 107.4 %all-reduce.8.cloned.1.call-done = f32[131072]{0:T(1024)} async-done(((f32[131072]{0:T(1024)}), f32[131072]{0:T(1024)}) %all-reduce.8.cloned.1.call-update) | async-done | bytes 524304 | tf_op jit(solution)/shard_map/psum | solution.py:47
  387.0 2.3 add_maximum_fusion
  389.2 0.8 copy.14
  (51 shorter events, 6.6 us)
Async XLA Ops:
  7.2 131.4 %all-reduce.4.cloned.1.call-start = ((), (), s32[]{:S(2)}) async-start(), calls=%async_computation | async-start | bytes 1048576 | tf_op jit(solution)/shard_map/psum | solution.py:47
  12.9 6.0 %copy-start = (bf16[40,128,128]{2,1,0:T(8,128)(2,1)S(1)}, bf16[40,128,128]{2,1,0:T(8,128)(2,1)}, u32[]{:S(2)}) copy-start(bf16[40,128,128]{2,1,0:T(8,128)(2,1)} %param.12) | copy-start | bytes 3932164
  12.9 6.0 %copy-start.1 = (bf16[40,128,128]{2,1,0:T(8,128)(2,1)S(1)}, bf16[40,128,128]{2,1,0:T(8,128)(2,1)}, u32[]{:S(2)}) copy-start(bf16[40,128,128]{2,1,0:T(8,128)(2,1)} %param.11) | copy-start | bytes 3932164
  18.9 1.7 copy-start.6
  24.0 114.6 %copy-start.2 = (f32[131072]{0:T(1024)S(1)}, f32[131072]{0:T(1024)}, u32[]{:S(2)}) copy-start(f32[131072]{0:T(1024)} %param.16) | copy-start | bytes 1572868
  27.5 234.8 %all-reduce.6.cloned.1.call-start = ((), (), s32[]{:S(2)}) async-start(), calls=%async_computation.1 | async-start | bytes 1048576 | tf_op jit(solution)/shard_map/psum | solution.py:47
  154.8 232.1 %all-reduce.8.cloned.1.call-start = ((), (), s32[]{:S(2)}) async-start(), calls=%async_computation.2 | async-start | bytes 1048576 | tf_op jit(solution)/shard_map/psum | solution.py:47
  277.7 109.3 %copy-start.3 = (f32[131072]{0:T(1024)S(1)}, f32[131072]{0:T(1024)}, u32[]{:S(2)}) copy-start(f32[131072]{0:T(1024)} %param.17) | copy-start | bytes 1572868
  277.7 109.3 %copy-start.4 = (f32[131072]{0:T(1024)S(1)}, f32[131072]{0:T(1024)}, u32[]{:S(2)}) copy-start(f32[131072]{0:T(1024)} %all-reduce.4.cloned.1.call-done) | copy-start | bytes 1572868
  387.0 2.3 copy-start.5
Sparse Core Ops, SparseCore 0:
  27.6 110.8 all-reduce.3
  154.9 107.2 all-reduce.5
  279.7 107.2 all-reduce.7
where the time goes:
time: 397 us
  waiting for transfers between devices  326 us (82%)
  other arithmetic  31.4 us (8%)
  blocking collectives  14.9 us (4%)
  between operations  14.6 us (4%)
  local copies, waits for them, and re-layouts  9.19 us (2%)
    psum x3, waiting for transfers between devices, local(): usage = lax.psum(local_use, 'mem')  326 us
  transfers between devices with their start and end apart: 3, of which 3 were waited for; matrix products, arithmetic and copies ran while one was open for 0% of the time, Pallas kernels for 0%

commit v1 on v0

v1 whole, which is shorter than its diff:
```python
import functools
import math

import jax
import jax.numpy as jnp
from jax import lax
from jax.experimental import pallas as pl
from jax.experimental.pallas import tpu as pltpu
from jax.sharding import PartitionSpec as P

MB = 8
ROUNDS = 3
SMOOTHING = 0.05
STEP_SIZE = 0.2
SCALE = math.log2(math.e) / SMOOTHING
MESH = pl.DeviceIdType.MESH
UNROLL = 2


def near_first(extent):
    return sorted(range(1, extent), key=lambda d: (min(d, extent - d), d))


def kernel(
    n_mem, n_camp, plane,
    gains, costs, rows, cols, count, duals, allowances,
    price_out, usage_out, unused_out,
    g_raw, c_raw, gain, cost, score, run, exp_cost, top_of, weight_of,
    pair, ids, picked, onehot, parts, price, usage, allow, spare, prev, last,
    load_sem, z_send, z_recv, p_send, p_recv, c_send, c_recv,
):
    slots, tile = gain.shape[0], gain.shape[1]
    blocks = price.shape[0]
    me = lax.axis_index("mem")
    me_c = lax.axis_index("camp")
    deep = n_mem // plane
    z, b = lax.div(me, plane), lax.rem(me, plane)

    loads = [
        pltpu.make_async_copy(src, dst, load_sem.at[i])
        for i, (src, dst) in enumerate(
            ((gains, g_raw), (costs, c_raw), (duals, price), (allowances, allow))
        )
    ]
    for load in loads:
        load.start()

    def z_peer(d):
        return {"mem": lax.rem(z + d, deep) * plane + b, "camp": me_c}

    def p_peer(e):
        return {"mem": z * plane + lax.rem(b + e, plane), "camp": me_c}

    def c_peer(f):
        return {"mem": me, "camp": lax.rem(me_c + f, n_camp)}

    def owner(d, e):
        return lax.rem(z - d + deep, deep) * plane + lax.rem(b - e + plane, plane)

    barrier = pltpu.get_barrier_semaphore()
    peers = (
        [z_peer(d) for d in range(1, deep)]
        + [p_peer(e) for e in range(1, plane)]
        + [c_peer(f) for f in range(1, n_camp)]
    )
    for peer in peers:
        pl.semaphore_signal(barrier, inc=1, device_id=peer, device_id_type=MESH)

    def link(s, lasts):
        row = rows[s, 0]
        live = s < count[0, 0]
        before = jnp.int32(0)
        after = []
        for k in range(MB):
            mine = row == k
            before = jnp.where(mine, lasts[k], before)
            after.append(jnp.where(mine & live, s + 1, lasts[k]))
        prev[s] = before
        block = jnp.where(live, cols[s, 0], -1)
        ids[me, pl.ds(s, 1), :] = jnp.full((1, tile), block, jnp.int32)
        return tuple(after)

    lasts = lax.fori_loop(0, slots, link, (jnp.int32(0),) * MB)
    for k in range(MB):
        last[k] = lasts[k]
    run[0] = jnp.zeros((tile, tile), jnp.float32)

    pl.semaphore_wait(barrier, len(peers))

    def z_copy(buf, t, d):
        return pltpu.make_async_remote_copy(
            buf.at[me], buf.at[me], z_send.at[t, d], z_recv.at[t, d], z_peer(d), MESH
        )

    def p_copy(buf, t, d, e):
        block = buf.at[owner(d, 0)]
        return pltpu.make_async_remote_copy(
            block, block, p_send.at[t, d, e], p_recv.at[t, d, e], p_peer(e), MESH
        )

    def gather_start(buf, t):
        for d in near_first(deep):
            z_copy(buf, t, d).start()
        for e in near_first(plane):
            p_copy(buf, t, 0, e).start()

    def gather_relay(buf, t):
        for d in near_first(deep):
            block = buf.at[owner(d, 0)]
            pltpu.make_async_remote_copy(
                block, block, z_send.at[t, d], z_recv.at[t, d], z_peer(d), MESH
            ).wait_recv()
            for e in near_first(plane):
                p_copy(buf, t, d, e).start()

    def gather_wait(buf, t):
        for d in [0] + near_first(deep):
            for e in near_first(plane):
                block = buf.at[owner(d, e)]
                pltpu.make_async_remote_copy(
                    block, block, p_send.at[t, d, e], p_recv.at[t, d, e], p_peer(e), MESH
                ).wait_recv()

    def gather_drain(buf, t):
        for d in near_first(deep):
            z_copy(buf, t, d).wait_send()
        for d in range(deep):
            for e in near_first(plane):
                p_copy(buf, t, d, e).wait_send()

    gather_start(ids, 0)

    loads[0].wait()
    loads[1].wait()

    def widen(s, _):
        gain[s] = g_raw[s].astype(jnp.float32) * SCALE
        cost[s] = c_raw[s].astype(jnp.float32)
        return 0

    lax.fori_loop(0, slots, widen, 0, unroll=UNROLL)
    loads[2].wait()
    loads[3].wait()
    lane = lax.broadcasted_iota(jnp.int32, (tile, tile), 1)

    def camp_copy(t, f):
        return pltpu.make_async_remote_copy(
            pair.at[t, me_c], pair.at[t, me_c], c_send.at[t, f], c_recv.at[t, f], c_peer(f), MESH
        )

    for t in range(ROUNDS):
        def scores(s, _):
            row_price = price[pl.ds(cols[s, 0], 1), :] * SCALE
            now = gain[s] - cost[s] * row_price
            score[s] = now
            run[s + 1] = jnp.maximum(run[prev[s]], now)
            return 0

        lax.fori_loop(0, slots, scores, 0, unroll=UNROLL)

        def tops(k, packed):
            top = jnp.max(run[last[k]], axis=1, keepdims=True)
            top = jnp.broadcast_to(top, (tile, tile))
            top_of[k] = top
            return jnp.where(lane == k, top, packed)

        packed = lax.fori_loop(0, MB, tops, jnp.zeros((tile, tile), jnp.float32))

        def exponents(s, _):
            now = jnp.exp2(score[s] - top_of[rows[s, 0]])
            exp_cost[s] = now * cost[s]
            run[s + 1] = run[prev[s]] + now
            return 0

        lax.fori_loop(0, slots, exponents, 0, unroll=UNROLL)

        def sums(k, packed):
            total = jnp.sum(run[last[k]], axis=1, keepdims=True)
            return jnp.where(lane == k + MB, total, packed)

        pair[t, me_c] = lax.fori_loop(0, MB, sums, packed)
        for f in range(1, n_camp):
            camp_copy(t, f).start()

        if t == 0:
            gather_relay(ids, 0)
            gather_wait(ids, 0)
            flat = ids[...].reshape(n_mem * slots, tile).astype(jnp.float32)
            id_row = jnp.transpose(flat)[0:1, :]

            def mark(j, _):
                first = pl.multiple_of(j * tile, tile)
                here = lax.broadcasted_iota(jnp.int32, (tile, n_mem * slots), 0) + first
                onehot[pl.ds(first, tile), :] = jnp.where(
                    here.astype(jnp.float32) == id_row, 1.0, 0.0
                ).astype(jnp.bfloat16)
                return 0

            lax.fori_loop(0, blocks // tile, mark, 0)

        for f in range(1, n_camp):
            block = pair.at[t, lax.rem(me_c - f + n_camp, n_camp)]
            pltpu.make_async_remote_copy(
                block, block, c_send.at[t, f], c_recv.at[t, f], c_peer(f), MESH
            ).wait_recv()

        mine = pair[t, me_c]
        top = pair[t, 0]
        for c in range(1, n_camp):
            top = jnp.maximum(top, pair[t, c])
        denom = jnp.zeros((tile, tile), jnp.float32)
        for c in range(n_camp):
            theirs = pair[t, c]
            denom = denom + jnp.exp2(theirs - top) * pltpu.roll(theirs, tile - MB, 1)
        left = jnp.exp2(-top)
        denom = left + denom
        weight = jnp.exp2(mine - top) / denom
        if t == ROUNDS - 1:
            spare[...] = jnp.transpose(left / denom)[:MB]
        for k in range(MB):
            weight_of[k] = jnp.broadcast_to(weight[:, k : k + 1], (tile, tile))

        def uses(s, _):
            used = jnp.sum(exp_cost[s] * weight_of[rows[s, 0]], axis=0, keepdims=True)
            picked[t, me, pl.ds(s, 1), :] = used
            return 0

        lax.fori_loop(0, slots, uses, 0, unroll=UNROLL)
        place = lax.broadcasted_iota(jnp.int32, (slots, tile), 0)
        picked[t, me] = jnp.where(place < count[0, 0], picked[t, me], 0.0)

        gather_start(picked.at[t], t + 1)
        gather_relay(picked.at[t], t + 1)
        gather_wait(picked.at[t], t + 1)

        rest = picked[t].reshape(n_mem * slots, tile)
        for i in range(3):
            part = rest.astype(jnp.bfloat16)
            parts[:, i * tile : (i + 1) * tile] = part
            rest = rest - part.astype(jnp.float32)

        def update(j, _):
            here = pl.ds(pl.multiple_of(j * tile, tile), tile)
            summed = jnp.dot(onehot[here, :], parts[...], preferred_element_type=jnp.float32)
            now = summed[:, :tile] + summed[:, tile : 2 * tile] + summed[:, 2 * tile :]
            usage[here, :] = now
            price[here, :] = jnp.maximum(price[here, :] + STEP_SIZE * (now - allow[here, :]), 0.0)
            return 0

        lax.fori_loop(0, blocks // tile, update, 0)

    stores = [
        pltpu.make_async_copy(src, dst, load_sem.at[i])
        for i, (src, dst) in enumerate(
            ((price, price_out), (usage, usage_out), (spare, unused_out))
        )
    ]
    for store in stores:
        store.start()
    gather_drain(ids, 0)
    for t in range(ROUNDS):
        gather_drain(picked.at[t], t + 1)
        for f in range(1, n_camp):
            camp_copy(t, f).wait_send()
    for store in stores:
        store.wait()


def local(n_mem, n_camp, gains, costs, tile_rows, tile_cols, tile_count, duals, allowances):
    slots, tile, _ = gains.shape
    blocks = duals.shape[0] // tile
    plane = 4 if n_mem % 4 == 0 else 1
    deep = n_mem // plane
    f32, bf16 = jnp.float32, jnp.bfloat16
    anywhere = pl.BlockSpec(memory_space=pl.ANY)
    scalar = pl.BlockSpec(memory_space=pltpu.SMEM)
    dma = pltpu.SemaphoreType.DMA
    price, usage, unused = pl.pallas_call(
        functools.partial(kernel, n_mem, n_camp, plane),
        out_shape=(
            jax.ShapeDtypeStruct((blocks, tile), f32),
            jax.ShapeDtypeStruct((blocks, tile), f32),
            jax.ShapeDtypeStruct((MB, tile), f32),
        ),
        in_specs=[anywhere, anywhere, scalar, scalar, scalar, anywhere, anywhere],
        out_specs=(anywhere,) * 3,
        scratch_shapes=[
            pltpu.VMEM((slots, tile, tile), bf16),
            pltpu.VMEM((slots, tile, tile), bf16),
            pltpu.VMEM((slots, tile, tile), f32),
            pltpu.VMEM((slots, tile, tile), f32),
            pltpu.VMEM((slots, tile, tile), f32),
            pltpu.VMEM((slots + 1, tile, tile), f32),
            pltpu.VMEM((slots, tile, tile), f32),
            pltpu.VMEM((MB, tile, tile), f32),
            pltpu.VMEM((MB, tile, tile), f32),
            pltpu.VMEM((ROUNDS, n_camp, tile, tile), f32),
            pltpu.VMEM((n_mem, slots, tile), jnp.int32),
            pltpu.VMEM((ROUNDS, n_mem, slots, tile), f32),
            pltpu.VMEM((blocks, n_mem * slots), bf16),
            pltpu.VMEM((n_mem * slots, 3 * tile), bf16),
            pltpu.VMEM((blocks, tile), f32),
            pltpu.VMEM((blocks, tile), f32),
            pltpu.VMEM((blocks, tile), f32),
            pltpu.VMEM((MB, tile), f32),
            pltpu.SMEM((slots,), jnp.int32),
            pltpu.SMEM((MB,), jnp.int32),
            dma((4,)),
            dma((ROUNDS + 1, deep)),
            dma((ROUNDS + 1, deep)),
            dma((ROUNDS + 1, deep, plane)),
            dma((ROUNDS + 1, deep, plane)),
            dma((ROUNDS, n_camp)),
            dma((ROUNDS, n_camp)),
        ],
        compiler_params=pltpu.CompilerParams(
            collective_id=0, has_side_effects=True, vmem_limit_bytes=56 * 1024 * 1024
        ),
    )(
        gains, costs, tile_rows, tile_cols, tile_count,
        duals.reshape(blocks, tile), allowances.reshape(blocks, tile),
    )
    return price.reshape(-1), usage.reshape(-1), unused.reshape(-1)


def solution(mesh):
    return jax.shard_map(
        functools.partial(local, mesh.shape["mem"], mesh.shape["camp"]),
        mesh=mesh,
        in_specs=(
            P("mem", None, "camp"),
            P("mem", None, "camp"),
            P("mem", "camp"),
            P("mem", "camp"),
            P("mem", "camp"),
            P("camp"),
            P("camp"),
        ),
        out_specs=(P("camp"), P("camp"), P("mem")),
        check_vma=False,
    )
```

time: 397 us -> 65.3 us (0.16)
  waiting for transfers between devices: 326 us -> 0 us
  Pallas kernels: 0 us -> 57.7 us
  other arithmetic: 31.4 us -> 0 us
  blocking collectives: 14.9 us -> 0 us
  between operations: 14.6 us -> 1.3 us
    psum x3 -> x0, waiting for transfers between devices: 326 us -> none  [local(): usage = lax.psum(local_use, 'mem')]
    pallas_call x0 -> x1, Pallas kernels: none -> 57.7 us  [local(): pl.pallas_call(functools.partial(kernel, n_mem, n_camp, plane), out_shape...]
    reduce_sum x6 -> x0, other arithmetic: 10.4 us -> none  [the longest x3 5.39 us: local(): jnp.sum(cost_f * alloc, axis=1)]
    gather x9 -> x0, local copies, waits for them, and re-layouts: 8.33 us -> none  [the longest x3 4.86 us: local(): price_tile = jnp.take(price.reshape(camp_blocks, tile), camp_block, axis=0)]
    pmax x3 -> x0, blocking collectives: 7.54 us -> none  [local(): row_top = lax.pmax(local_top, 'camp')]
    psum x3 -> x0, blocking collectives: 7.39 us -> none  [local(): row_sum = lax.psum(local_sum, 'camp')]
    scatter-add x3 -> x0, other arithmetic: 5.23 us -> none  [local(): jax.ops.segment_sum(column_use, camp_block, num_segments=camp_blocks)]
    unnamed x15 -> x9, local copies, waits for them, and re-layouts: 0.86 us -> 6.04 us
  transfers between devices with their start and end apart: 3 -> 0, of which waited for: 3 -> 0; matrix products, arithmetic and copies ran while one was open for 0% -> 0% of each run, Pallas kernels for 0% -> 0%
where the time goes in v1:
time: 65.3 us; the launch traced here: 65.1 us
  Pallas kernels  57.7 us (88%)
  local copies, waits for them, and re-layouts  6.04 us (9%)
  between operations  1.3 us (2%)
    pallas_call x1, Pallas kernels, local(): pl.pallas_call(functools.partial(kernel, n_mem, n_camp, plane), out_shape...  57.7 us
    unnamed x9, local copies, waits for them, and re-layouts  6.04 us

profile of v1, /device:TPU:0, one launch (start us, length us, event | category | flops | bytes accessed | tf_op | source)
XLA Modules:
  0.0 65.1 jit_solution(16700161113136675318)
XLA Ops:
  1.3 1.3 %copy.10.rows = s32[40,1]{1,0:T(8,128)} copy(s32[40,1]{0,1:T(1,128)} %param.9) | data formatting | bytes 320 | tf_op args[2]
  2.6 1.3 %copy.11.cols = s32[40,1]{1,0:T(8,128)} copy(s32[40,1]{0,1:T(1,128)} %param.10) | data formatting | bytes 320 | tf_op args[3]
  4.0 57.7 %shard_map.94 = (f32[1024,128]{1,0:T(8,128)}, f32[1024,128]{1,0:T(8,128)}, f32[8,128]{1,0:T(8,128)}) custom-call(bf16[40,128,128]{2,1,0:T(8,128)(2,1)} %gains.1, bf16[40,128,128]{2,1,0:T(8,128)(2,1)} %costs.1, s32[40,1]{1,0:T(8,128)} %copy.10.rows, s32[40,1]{1,0:T(8,128)} %copy.11.cols, s32[1,1]{1,0:T(1,128)S(6)} %copy.15.count, f32[1024,128]{1,0:T(8,128)} %bitcast.7, ...), custom_call_target="tpu_custom_call" | custom-call | tf_op jit(solution)/shard_map/pallas_call | solution.py:278
  61.7 0.0 copy-start
  61.7 0.0 copy-start.1
  61.7 1.9 %copy.16 = f32[131072]{0:T(1024)} copy(f32[131072]{0:T(1024)} %bitcast.6) | data formatting | bytes 1048576
  63.6 0.0 copy-done
  63.6 0.8 %copy.17 = f32[131072]{0:T(1024)} copy(f32[131072]{0:T(1024)S(1)} %bitcast.5) | data formatting | bytes 1048576
  64.5 0.0 copy-done.1
  64.5 0.6 copy.18
Async XLA Ops:
  61.7 1.9 %copy-start = (f32[1024,128]{1,0:T(8,128)S(1)}, f32[1024,128]{1,0:T(8,128)}, u32[]{:S(2)}) copy-start(f32[1024,128]{1,0:T(8,128)} %get-tuple-element.7) | copy-start | bytes 1572868
  61.7 2.8 %copy-start.1 = (f32[8,128]{1,0:T(8,128)S(1)}, f32[8,128]{1,0:T(8,128)}, u32[]{:S(2)}) copy-start(f32[8,128]{1,0:T(8,128)} %get-tuple-element.8) | copy-start | bytes 12292

commit v2 on v1

--- a/solution.py
+++ b/solution.py
@@ -14,7 +14,7 @@
 STEP_SIZE = 0.2
 SCALE = math.log2(math.e) / SMOOTHING
 MESH = pl.DeviceIdType.MESH
-UNROLL = 2
+UNROLL = 8
 
 
 def near_first(extent):
@@ -24,9 +24,9 @@
 def kernel(
     n_mem, n_camp, plane,
     gains, costs, rows, cols, count, duals, allowances,
-    price_out, usage_out, unused_out,
+    price, usage, spare,
     g_raw, c_raw, gain, cost, score, run, exp_cost, top_of, weight_of,
-    pair, ids, picked, onehot, parts, price, usage, allow, spare, prev, last,
+    pair, ids, picked, onehot, parts, allow, prev, last,
     load_sem, z_send, z_recv, p_send, p_recv, c_send, c_recv,
 ):
     slots, tile = gain.shape[0], gain.shape[1]
@@ -67,7 +67,7 @@
         pl.semaphore_signal(barrier, inc=1, device_id=peer, device_id_type=MESH)
 
     def link(s, lasts):
-        row = rows[s, 0]
+        row = rows[0, s]
         live = s < count[0, 0]
         before = jnp.int32(0)
         after = []
@@ -76,7 +76,7 @@
             before = jnp.where(mine, lasts[k], before)
             after.append(jnp.where(mine & live, s + 1, lasts[k]))
         prev[s] = before
-        block = jnp.where(live, cols[s, 0], -1)
+        block = jnp.where(live, cols[0, s], -1)
         ids[me, pl.ds(s, 1), :] = jnp.full((1, tile), block, jnp.int32)
         return tuple(after)
 
@@ -133,12 +133,6 @@
     loads[0].wait()
     loads[1].wait()
 
-    def widen(s, _):
-        gain[s] = g_raw[s].astype(jnp.float32) * SCALE
-        cost[s] = c_raw[s].astype(jnp.float32)
-        return 0
-
-    lax.fori_loop(0, slots, widen, 0, unroll=UNROLL)
     loads[2].wait()
     loads[3].wait()
     lane = lax.broadcasted_iota(jnp.int32, (tile, tile), 1)
@@ -150,8 +144,15 @@
 
     for t in range(ROUNDS):
         def scores(s, _):
-            row_price = price[pl.ds(cols[s, 0], 1), :] * SCALE
-            now = gain[s] - cost[s] * row_price
+            row_price = price[pl.ds(cols[0, s], 1), :] * SCALE
+            if t == 0:
+                worth = g_raw[s].astype(jnp.float32) * SCALE
+                drawn = c_raw[s].astype(jnp.float32)
+                gain[s] = worth
+                cost[s] = drawn
+            else:
+                worth, drawn = gain[s], cost[s]
+            now = worth - drawn * row_price
             score[s] = now
             run[s + 1] = jnp.maximum(run[prev[s]], now)
             return 0
@@ -164,10 +165,10 @@
             top_of[k] = top
             return jnp.where(lane == k, top, packed)
 
-        packed = lax.fori_loop(0, MB, tops, jnp.zeros((tile, tile), jnp.float32))
+        packed = lax.fori_loop(0, MB, tops, jnp.zeros((tile, tile), jnp.float32), unroll=MB)
 
         def exponents(s, _):
-            now = jnp.exp2(score[s] - top_of[rows[s, 0]])
+            now = jnp.exp2(score[s] - top_of[rows[0, s]])
             exp_cost[s] = now * cost[s]
             run[s + 1] = run[prev[s]] + now
             return 0
@@ -178,7 +179,7 @@
             total = jnp.sum(run[last[k]], axis=1, keepdims=True)
             return jnp.where(lane == k + MB, total, packed)
 
-        pair[t, me_c] = lax.fori_loop(0, MB, sums, packed)
+        pair[t, me_c] = lax.fori_loop(0, MB, sums, packed, unroll=MB)
         for f in range(1, n_camp):
             camp_copy(t, f).start()
 
@@ -221,7 +222,7 @@
             weight_of[k] = jnp.broadcast_to(weight[:, k : k + 1], (tile, tile))
 
         def uses(s, _):
-            used = jnp.sum(exp_cost[s] * weight_of[rows[s, 0]], axis=0, keepdims=True)
+            used = jnp.sum(exp_cost[s] * weight_of[rows[0, s]], axis=0, keepdims=True)
             picked[t, me, pl.ds(s, 1), :] = used
             return 0
 
@@ -239,29 +240,27 @@
             parts[:, i * tile : (i + 1) * tile] = part
             rest = rest - part.astype(jnp.float32)
 
-        def update(j, _):
-            here = pl.ds(pl.multiple_of(j * tile, tile), tile)
-            summed = jnp.dot(onehot[here, :], parts[...], preferred_element_type=jnp.float32)
-            now = summed[:, :tile] + summed[:, tile : 2 * tile] + summed[:, 2 * tile :]
-            usage[here, :] = now
-            price[here, :] = jnp.maximum(price[here, :] + STEP_SIZE * (now - allow[here, :]), 0.0)
-            return 0
-
-        lax.fori_loop(0, blocks // tile, update, 0)
-
-    stores = [
-        pltpu.make_async_copy(src, dst, load_sem.at[i])
-        for i, (src, dst) in enumerate(
-            ((price, price_out), (usage, usage_out), (spare, unused_out))
-        )
-    ]
-    for store in stores:
-        store.start()
+        summed = jnp.dot(onehot[...], parts[...], preferred_element_type=jnp.float32)
+        now = summed[:, :tile] + summed[:, tile : 2 * tile] + summed[:, 2 * tile :]
+        usage[...] = now
+        price[...] = jnp.maximum(price[...] + STEP_SIZE * (now - allow[...]), 0.0)
+
     gather_drain(ids, 0)
     for t in range(ROUNDS):
         gather_drain(picked.at[t], t + 1)
         for f in range(1, n_camp):
             camp_copy(t, f).wait_send()
+
+
+def hand_over(price, usage, spare, price_out, usage_out, unused_out, sem):
+    stores = [
+        pltpu.make_async_copy(src, dst, sem.at[i])
+        for i, (src, dst) in enumerate(
+            ((price, price_out), (usage, usage_out), (spare, unused_out))
+        )
+    ]
+    for store in stores:
+        store.start()
     for store in stores:
         store.wait()
 
@@ -275,15 +274,12 @@
     anywhere = pl.BlockSpec(memory_space=pl.ANY)
     scalar = pl.BlockSpec(memory_space=pltpu.SMEM)
     dma = pltpu.SemaphoreType.DMA
-    price, usage, unused = pl.pallas_call(
+    shapes = ((blocks, tile), (blocks, tile), (MB, tile))
+    held = pl.pallas_call(
         functools.partial(kernel, n_mem, n_camp, plane),
-        out_shape=(
-            jax.ShapeDtypeStruct((blocks, tile), f32),
-            jax.ShapeDtypeStruct((blocks, tile), f32),
-            jax.ShapeDtypeStruct((MB, tile), f32),
-        ),
+        out_shape=tuple(pltpu.VMEM(shape, f32) for shape in shapes),
         in_specs=[anywhere, anywhere, scalar, scalar, scalar, anywhere, anywhere],
-        out_specs=(anywhere,) * 3,
+        out_specs=(pl.BlockSpec(memory_space=pltpu.VMEM),) * 3,
         scratch_shapes=[
             pltpu.VMEM((slots, tile, tile), bf16),
             pltpu.VMEM((slots, tile, tile), bf16),
@@ -300,9 +296,6 @@
             pltpu.VMEM((blocks, n_mem * slots), bf16),
             pltpu.VMEM((n_mem * slots, 3 * tile), bf16),
             pltpu.VMEM((blocks, tile), f32),
-            pltpu.VMEM((blocks, tile), f32),
-            pltpu.VMEM((blocks, tile), f32),
-            pltpu.VMEM((MB, tile), f32),
             pltpu.SMEM((slots,), jnp.int32),
             pltpu.SMEM((MB,), jnp.int32),
             dma((4,)),
@@ -317,9 +310,16 @@
             collective_id=0, has_side_effects=True, vmem_limit_bytes=56 * 1024 * 1024
         ),
     )(
-        gains, costs, tile_rows, tile_cols, tile_count,
+        gains, costs, tile_rows.T, tile_cols.T, tile_count,
         duals.reshape(blocks, tile), allowances.reshape(blocks, tile),
     )
+    price, usage, unused = pl.pallas_call(
+        hand_over,
+        out_shape=tuple(jax.ShapeDtypeStruct(shape, f32) for shape in shapes),
+        in_specs=[pl.BlockSpec(memory_space=pltpu.VMEM)] * 3,
+        out_specs=(anywhere,) * 3,
+        scratch_shapes=[dma((3,))],
+    )(*held)
     return price.reshape(-1), usage.reshape(-1), unused.reshape(-1)
 
 

time: 65.3 us -> 55.1 us (0.84)
  Pallas kernels: 57.7 us -> 51.5 us
  local copies, waits for them, and re-layouts: 6.04 us -> 2.18 us
    pallas_call x1, Pallas kernels: 57.7 us -> 49.3 us  [local(): pl.pallas_call(functools.partial(kernel, n_mem, n_camp, plane), out_shape...]
    unnamed x9 -> x6, local copies, waits for them, and re-layouts: 6.04 us -> 2.18 us
    pallas_call x0 -> x1, Pallas kernels: none -> 2.19 us  [local(): pl.pallas_call(hand_over, out_shape=tuple((jax.ShapeDtypeStruct(shape, f3...]
where the time goes in v2:
time: 55.1 us; the launch traced here: 54.9 us
  Pallas kernels  51.5 us (93%)
  local copies, waits for them, and re-layouts  2.18 us (4%)
  between operations  1.3 us (2%)
    pallas_call x1, Pallas kernels, local(): pl.pallas_call(functools.partial(kernel, n_mem, n_camp, plane), out_shape...  49.3 us
    pallas_call x1, Pallas kernels, local(): pl.pallas_call(hand_over, out_shape=tuple((jax.ShapeDtypeStruct(shape, f3...  2.19 us
    unnamed x6, local copies, waits for them, and re-layouts  2.18 us

profile of v2, /device:TPU:0, one launch (start us, length us, event | category | flops | bytes accessed | tf_op | source)
XLA Modules:
  0.0 54.9 jit_solution(1316750127566995310)
XLA Ops:
  1.3 49.3 %shard_map.94 = (f32[1024,128]{1,0:T(8,128)S(1)}, f32[1024,128]{1,0:T(8,128)S(1)}, f32[8,128]{1,0:T(8,128)S(1)}) custom-call(bf16[40,128,128]{2,1,0:T(8,128)(2,1)} %gains.1, bf16[40,128,128]{2,1,0:T(8,128)(2,1)} %costs.1, s32[1,40]{1,0:T(1,128)} %bitcast.9, s32[1,40]{1,0:T(1,128)} %bitcast.10, s32[1,1]{1,0:T(1,128)S(6)} %copy.10.count, f32[1024,128]{1,0:T(8,128)} %bitcast.7, ...), custom_call_target="tpu_custom_call" | custom-call | tf_op jit(solution)/shard_map/pallas_call | solution.py:278
  50.6 0.0 copy-start
  50.6 0.8 %copy-done = f32[1024,128]{1,0:T(8,128)} copy-done((f32[1024,128]{1,0:T(8,128)}, f32[1024,128]{1,0:T(8,128)S(1)}, u32[]{:S(2)}) %copy-start) | copy-done | bytes 524312
  51.4 0.0 copy-start.1
  51.4 0.8 %copy-done.1 = f32[1024,128]{1,0:T(8,128)} copy-done((f32[1024,128]{1,0:T(8,128)}, f32[1024,128]{1,0:T(8,128)S(1)}, u32[]{:S(2)}) %copy-start.1) | copy-done | bytes 524312
  52.2 0.0 copy-start.2
  52.2 0.6 %copy-done.2 = f32[8,128]{1,0:T(8,128)} copy-done((f32[8,128]{1,0:T(8,128)}, f32[8,128]{1,0:T(8,128)S(1)}, u32[]{:S(2)}) %copy-start.2) | copy-done | bytes 4120
  52.8 2.2 %shard_map.95 = (f32[1024,128]{1,0:T(8,128)}, f32[1024,128]{1,0:T(8,128)}, f32[8,128]{1,0:T(8,128)}) custom-call(f32[1024,128]{1,0:T(8,128)} %copy-done, f32[1024,128]{1,0:T(8,128)} %copy-done.1, f32[8,128]{1,0:T(8,128)} %copy-done.2), custom_call_target="tpu_custom_call" | custom-call | tf_op jit(solution)/shard_map/pallas_call | solution.py:316
Async XLA Ops:
  50.6 0.8 %copy-start = (f32[1024,128]{1,0:T(8,128)}, f32[1024,128]{1,0:T(8,128)S(1)}, u32[]{:S(2)}) copy-start(f32[1024,128]{1,0:T(8,128)S(1)} %get-tuple-element.9.price) | copy-start | bytes 1572868
  51.4 0.8 %copy-start.1 = (f32[1024,128]{1,0:T(8,128)}, f32[1024,128]{1,0:T(8,128)S(1)}, u32[]{:S(2)}) copy-start(f32[1024,128]{1,0:T(8,128)S(1)} %get-tuple-element.10.usage) | copy-start | bytes 1572868
  52.2 0.6 %copy-start.2 = (f32[8,128]{1,0:T(8,128)}, f32[8,128]{1,0:T(8,128)S(1)}, u32[]{:S(2)}) copy-start(f32[8,128]{1,0:T(8,128)S(1)} %get-tuple-element.11.spare) | copy-start | bytes 12292

commit v3 on v2

--- a/solution.py
+++ b/solution.py
@@ -17,8 +17,13 @@
 UNROLL = 8
 
 
-def near_first(extent):
-    return sorted(range(1, extent), key=lambda d: (min(d, extent - d), d))
+def flip(i, d):
+    out, bit = i, 1
+    while bit <= d:
+        if d & bit:
+            out = out + bit - 2 * bit * lax.rem(lax.div(i, bit), 2)
+        bit *= 2
+    return out
 
 
 def kernel(
@@ -26,7 +31,8 @@
     gains, costs, rows, cols, count, duals, allowances,
     price, usage, spare,
     g_raw, c_raw, gain, cost, score, run, exp_cost, top_of, weight_of,
-    pair, ids, picked, onehot, parts, allow, prev, last,
+    pair, ids, picked, onehot, own_hot, parts, allow,
+    own_id, own_price, own_allow, prev, last,
     load_sem, z_send, z_recv, p_send, p_recv, c_send, c_recv,
 ):
     slots, tile = gain.shape[0], gain.shape[1]
@@ -46,16 +52,16 @@
         load.start()
 
     def z_peer(d):
-        return {"mem": lax.rem(z + d, deep) * plane + b, "camp": me_c}
+        return {"mem": flip(z, d) * plane + b, "camp": me_c}
 
     def p_peer(e):
-        return {"mem": z * plane + lax.rem(b + e, plane), "camp": me_c}
+        return {"mem": z * plane + flip(b, e), "camp": me_c}
 
     def c_peer(f):
         return {"mem": me, "camp": lax.rem(me_c + f, n_camp)}
 
     def owner(d, e):
-        return lax.rem(z - d + deep, deep) * plane + lax.rem(b - e + plane, plane)
+        return flip(z, d) * plane + flip(b, e)
 
     barrier = pltpu.get_barrier_semaphore()
     peers = (
@@ -66,7 +72,12 @@
     for peer in peers:
         pl.semaphore_signal(barrier, inc=1, device_id=peer, device_id_type=MESH)
 
-    def link(s, lasts):
+    id_rows = ids.shape[1]
+    spot = lax.broadcasted_iota(jnp.int32, (id_rows, tile), 0) * tile
+    spot = spot + lax.broadcasted_iota(jnp.int32, (id_rows, tile), 1) - me * slots
+
+    def link(s, carry):
+        lasts, packed = carry
         row = rows[0, s]
         live = s < count[0, 0]
         before = jnp.int32(0)
@@ -76,16 +87,17 @@
             before = jnp.where(mine, lasts[k], before)
             after.append(jnp.where(mine & live, s + 1, lasts[k]))
         prev[s] = before
-        block = jnp.where(live, cols[0, s], -1)
-        ids[me, pl.ds(s, 1), :] = jnp.full((1, tile), block, jnp.int32)
-        return tuple(after)
-
-    lasts = lax.fori_loop(0, slots, link, (jnp.int32(0),) * MB)
+        block = jnp.where(live, cols[0, s] + 1, 0)
+        own_id[pl.ds(s, 1), :] = jnp.full((1, tile), block, jnp.int32)
+        return tuple(after), jnp.where(spot == s, block, packed)
+
+    lasts, packed_ids = lax.fori_loop(
+        0, slots, link, ((jnp.int32(0),) * MB, jnp.zeros((id_rows, tile), jnp.int32)), unroll=4
+    )
+    ids[me] = packed_ids
     for k in range(MB):
         last[k] = lasts[k]
     run[0] = jnp.zeros((tile, tile), jnp.float32)
-
-    pl.semaphore_wait(barrier, len(peers))
 
     def z_copy(buf, t, d):
         return pltpu.make_async_remote_copy(
@@ -99,42 +111,47 @@
         )
 
     def gather_start(buf, t):
-        for d in near_first(deep):
+        for d in range(1, deep):
             z_copy(buf, t, d).start()
-        for e in near_first(plane):
+        for e in range(1, plane):
             p_copy(buf, t, 0, e).start()
 
     def gather_relay(buf, t):
-        for d in near_first(deep):
+        for d in range(1, deep):
             block = buf.at[owner(d, 0)]
             pltpu.make_async_remote_copy(
                 block, block, z_send.at[t, d], z_recv.at[t, d], z_peer(d), MESH
             ).wait_recv()
-            for e in near_first(plane):
+            for e in range(1, plane):
                 p_copy(buf, t, d, e).start()
 
     def gather_wait(buf, t):
-        for d in [0] + near_first(deep):
-            for e in near_first(plane):
+        for d in range(deep):
+            for e in range(1, plane):
                 block = buf.at[owner(d, e)]
                 pltpu.make_async_remote_copy(
                     block, block, p_send.at[t, d, e], p_recv.at[t, d, e], p_peer(e), MESH
                 ).wait_recv()
 
     def gather_drain(buf, t):
-        for d in near_first(deep):
+        for d in range(1, deep):
             z_copy(buf, t, d).wait_send()
         for d in range(deep):
-            for e in near_first(plane):
+            for e in range(1, plane):
                 p_copy(buf, t, d, e).wait_send()
 
-    gather_start(ids, 0)
-
+    loads[2].wait()
+    loads[3].wait()
+
+    def fetch(s, _):
+        here = pl.ds(cols[0, s], 1)
+        own_price[pl.ds(s, 1), :] = price[here, :]
+        own_allow[pl.ds(s, 1), :] = allow[here, :]
+        return 0
+
+    lax.fori_loop(0, slots, fetch, 0, unroll=UNROLL)
     loads[0].wait()
     loads[1].wait()
-
-    loads[2].wait()
-    loads[3].wait()
     lane = lax.broadcasted_iota(jnp.int32, (tile, tile), 1)
 
     def camp_copy(t, f):
@@ -142,9 +159,36 @@
             pair.at[t, me_c], pair.at[t, me_c], c_send.at[t, f], c_recv.at[t, f], c_peer(f), MESH
         )
 
+    def mark():
+        packed = ids[0]
+        for p in range(1, n_mem):
+            packed = packed + ids[p]
+        for i in range(n_mem * slots // tile):
+            id_row = packed[i : i + 1, :]
+            own_hot[:, i * tile : (i + 1) * tile] = jnp.where(
+                own_id[...] == id_row, 1.0, 0.0
+            ).astype(jnp.bfloat16)
+            for j in range(blocks // tile):
+                here = lax.broadcasted_iota(jnp.int32, (tile, tile), 0) + (j * tile + 1)
+                onehot[j * tile : (j + 1) * tile, i * tile : (i + 1) * tile] = jnp.where(
+                    here == id_row, 1.0, 0.0
+                ).astype(jnp.bfloat16)
+
+    def summed_by(hot):
+        three = jnp.dot(hot, parts[...], preferred_element_type=jnp.float32)
+        return three[:, :tile] + three[:, tile : 2 * tile] + three[:, 2 * tile :]
+
+    def advance(price, used, allow):
+        return jnp.maximum(price + STEP_SIZE * (used - allow), 0.0)
+
+    def dense():
+        now = summed_by(onehot[...])
+        usage[...] = now
+        price[...] = advance(price[...], now, allow[...])
+
     for t in range(ROUNDS):
         def scores(s, _):
-            row_price = price[pl.ds(cols[0, s], 1), :] * SCALE
+            row_price = own_price[pl.ds(s, 1), :] * SCALE
             if t == 0:
                 worth = g_raw[s].astype(jnp.float32) * SCALE
                 drawn = c_raw[s].astype(jnp.float32)
@@ -158,6 +202,9 @@
             return 0
 
         lax.fori_loop(0, slots, scores, 0, unroll=UNROLL)
+        if t == 0:
+            pl.semaphore_wait(barrier, len(peers))
+            gather_start(ids, 0)
 
         def tops(k, packed):
             top = jnp.max(run[last[k]], axis=1, keepdims=True)
@@ -185,19 +232,8 @@
 
         if t == 0:
             gather_relay(ids, 0)
-            gather_wait(ids, 0)
-            flat = ids[...].reshape(n_mem * slots, tile).astype(jnp.float32)
-            id_row = jnp.transpose(flat)[0:1, :]
-
-            def mark(j, _):
-                first = pl.multiple_of(j * tile, tile)
-                here = lax.broadcasted_iota(jnp.int32, (tile, n_mem * slots), 0) + first
-                onehot[pl.ds(first, tile), :] = jnp.where(
-                    here.astype(jnp.float32) == id_row, 1.0, 0.0
-                ).astype(jnp.bfloat16)
-                return 0
-
-            lax.fori_loop(0, blocks // tile, mark, 0)
+        else:
+            dense()
 
         for f in range(1, n_camp):
             block = pair.at[t, lax.rem(me_c - f + n_camp, n_camp)]
@@ -232,6 +268,9 @@
 
         gather_start(picked.at[t], t + 1)
         gather_relay(picked.at[t], t + 1)
+        if t == 0:
+            gather_wait(ids, 0)
+            mark()
         gather_wait(picked.at[t], t + 1)
 
         rest = picked[t].reshape(n_mem * slots, tile)
@@ -240,10 +279,10 @@
             parts[:, i * tile : (i + 1) * tile] = part
             rest = rest - part.astype(jnp.float32)
 
-        summed = jnp.dot(onehot[...], parts[...], preferred_element_type=jnp.float32)
-        now = summed[:, :tile] + summed[:, tile : 2 * tile] + summed[:, 2 * tile :]
-        usage[...] = now
-        price[...] = jnp.maximum(price[...] + STEP_SIZE * (now - allow[...]), 0.0)
+        if t < ROUNDS - 1:
+            own_price[...] = advance(own_price[...], summed_by(own_hot[...]), own_allow[...])
+        else:
+            dense()
 
     gather_drain(ids, 0)
     for t in range(ROUNDS):
@@ -270,6 +309,7 @@
     blocks = duals.shape[0] // tile
     plane = 4 if n_mem % 4 == 0 else 1
     deep = n_mem // plane
+    id_rows = -(-n_mem * slots // (8 * tile)) * 8
     f32, bf16 = jnp.float32, jnp.bfloat16
     anywhere = pl.BlockSpec(memory_space=pl.ANY)
     scalar = pl.BlockSpec(memory_space=pltpu.SMEM)
@@ -291,11 +331,15 @@
             pltpu.VMEM((MB, tile, tile), f32),
             pltpu.VMEM((MB, tile, tile), f32),
             pltpu.VMEM((ROUNDS, n_camp, tile, tile), f32),
-            pltpu.VMEM((n_mem, slots, tile), jnp.int32),
+            pltpu.VMEM((n_mem, id_rows, tile), jnp.int32),
             pltpu.VMEM((ROUNDS, n_mem, slots, tile), f32),
             pltpu.VMEM((blocks, n_mem * slots), bf16),
+            pltpu.VMEM((slots, n_mem * slots), bf16),
             pltpu.VMEM((n_mem * slots, 3 * tile), bf16),
             pltpu.VMEM((blocks, tile), f32),
+            pltpu.VMEM((slots, tile), jnp.int32),
+            pltpu.VMEM((slots, tile), f32),
+            pltpu.VMEM((slots, tile), f32),
             pltpu.SMEM((slots,), jnp.int32),
             pltpu.SMEM((MB,), jnp.int32),
             dma((4,)),
@@ -307,7 +351,7 @@
             dma((ROUNDS, n_camp)),
         ],
         compiler_params=pltpu.CompilerParams(
-            collective_id=0, has_side_effects=True, vmem_limit_bytes=56 * 1024 * 1024
+            collective_id=0, has_side_effects=True, vmem_limit_bytes=44 * 1024 * 1024
         ),
     )(
         gains, costs, tile_rows.T, tile_cols.T, tile_count,
@@ -319,6 +363,7 @@
         in_specs=[pl.BlockSpec(memory_space=pltpu.VMEM)] * 3,
         out_specs=(anywhere,) * 3,
         scratch_shapes=[dma((3,))],
+        compiler_params=pltpu.CompilerParams(vmem_limit_bytes=1024 * 1024),
     )(*held)
     return price.reshape(-1), usage.reshape(-1), unused.reshape(-1)
 

time: 55.1 us -> 52.2 us (0.947)
  Pallas kernels: 51.5 us -> 44.6 us
  local copies, waits for them, and re-layouts: 2.18 us -> 6.02 us
    pallas_call x1, Pallas kernels: 49.3 us -> 43.6 us  [local(): pl.pallas_call(functools.partial(kernel, n_mem, n_camp, plane), out_shape...]
    unnamed x6 -> x12, local copies, waits for them, and re-layouts: 2.18 us -> 6.02 us
    pallas_call x1, Pallas kernels: 2.19 us -> 1 us  [local(): pl.pallas_call(hand_over, out_shape=tuple((jax.ShapeDtypeStruct(shape, f3...]
where the time goes in v3:
time: 52.2 us; the launch traced here: 51.9 us
  Pallas kernels  44.6 us (85%)
  local copies, waits for them, and re-layouts  6.02 us (12%)
  between operations  1.3 us (2%)
    pallas_call x1, Pallas kernels, local(): pl.pallas_call(functools.partial(kernel, n_mem, n_camp, plane), out_shape...  43.6 us
    unnamed x12, local copies, waits for them, and re-layouts  6.02 us

profile of v3, /device:TPU:0, one launch (start us, length us, event | category | flops | bytes accessed | tf_op | source)
XLA Modules:
  0.0 51.9 jit_solution(7879669964618257531)
XLA Ops:
  1.3 0.0 copy-start
  1.3 1.3 %copy-done = bf16[40,128,128]{2,1,0:T(8,128)(2,1)S(1)} copy-done((bf16[40,128,128]{2,1,0:T(8,128)(2,1)S(1)}, bf16[40,128,128]{2,1,0:T(8,128)(2,1)}, u32[]{:S(2)}) %copy-start) | copy-done | bytes 1310744
  2.6 0.0 copy-start.1
  2.6 1.3 %copy-done.1 = bf16[40,128,128]{2,1,0:T(8,128)(2,1)S(1)} copy-done((bf16[40,128,128]{2,1,0:T(8,128)(2,1)S(1)}, bf16[40,128,128]{2,1,0:T(8,128)(2,1)}, u32[]{:S(2)}) %copy-start.1) | copy-done | bytes 1310744
  3.9 0.0 copy-start.2
  3.9 1.0 %copy-done.2 = f32[131072]{0:T(1024)S(1)} copy-done((f32[131072]{0:T(1024)S(1)}, f32[131072]{0:T(1024)}, u32[]{:S(2)}) %copy-start.2) | copy-done | bytes 524312
  5.0 0.0 copy-start.3
  5.0 1.0 %copy-done.3 = f32[131072]{0:T(1024)S(1)} copy-done((f32[131072]{0:T(1024)S(1)}, f32[131072]{0:T(1024)}, u32[]{:S(2)}) %copy-start.3) | copy-done | bytes 524312
  6.0 0.0 copy-start.4
  6.0 0.7 %copy-done.4 = s32[40,1]{0,1:T(1,128)S(1)} copy-done((s32[40,1]{0,1:T(1,128)S(1)}, s32[40,1]{0,1:T(1,128)}, u32[]{:S(2)}) %copy-start.4) | copy-done | bytes 184
  6.7 0.0 copy-start.5
  6.7 0.7 %copy-done.5 = s32[40,1]{0,1:T(1,128)S(1)} copy-done((s32[40,1]{0,1:T(1,128)S(1)}, s32[40,1]{0,1:T(1,128)}, u32[]{:S(2)}) %copy-start.5) | copy-done | bytes 184
  7.3 43.6 %shard_map.94 = (f32[1024,128]{1,0:T(8,128)S(1)}, f32[1024,128]{1,0:T(8,128)S(1)}, f32[8,128]{1,0:T(8,128)S(1)}) custom-call(bf16[40,128,128]{2,1,0:T(8,128)(2,1)S(1)} %copy-done, bf16[40,128,128]{2,1,0:T(8,128)(2,1)S(1)} %copy-done.1, s32[1,40]{1,0:T(1,128)S(1)} %bitcast.9, s32[1,40]{1,0:T(1,128)S(1)} %bitcast.10, s32[1,1]{1,0:T(1,128)S(6)} %copy.10.count, ...), custom_call_target="tpu_custom_call" | custom-call | tf_op jit(solution)/shard_map/pallas_call | solution.py:318
  50.9 1.0 %shard_map.95 = (f32[1024,128]{1,0:T(8,128)}, f32[1024,128]{1,0:T(8,128)}, f32[8,128]{1,0:T(8,128)}) custom-call(f32[1024,128]{1,0:T(8,128)S(1)} %get-tuple-element.9.price, f32[1024,128]{1,0:T(8,128)S(1)} %get-tuple-element.10.usage, f32[8,128]{1,0:T(8,128)S(1)} %get-tuple-element.11.spare), custom_call_target="tpu_custom_call" | custom-call | tf_op jit(solution)/shard_map/pallas_call | solution.py:360
Async XLA Ops:
  1.3 1.3 %copy-start = (bf16[40,128,128]{2,1,0:T(8,128)(2,1)S(1)}, bf16[40,128,128]{2,1,0:T(8,128)(2,1)}, u32[]{:S(2)}) copy-start(bf16[40,128,128]{2,1,0:T(8,128)(2,1)} %gains.1) | copy-start | bytes 3932164
  2.6 1.3 %copy-start.1 = (bf16[40,128,128]{2,1,0:T(8,128)(2,1)S(1)}, bf16[40,128,128]{2,1,0:T(8,128)(2,1)}, u32[]{:S(2)}) copy-start(bf16[40,128,128]{2,1,0:T(8,128)(2,1)} %costs.1) | copy-start | bytes 3932164
  3.9 1.0 %copy-start.2 = (f32[131072]{0:T(1024)S(1)}, f32[131072]{0:T(1024)}, u32[]{:S(2)}) copy-start(f32[131072]{0:T(1024)} %param.12) | copy-start | bytes 1572868
  5.0 1.0 %copy-start.3 = (f32[131072]{0:T(1024)S(1)}, f32[131072]{0:T(1024)}, u32[]{:S(2)}) copy-start(f32[131072]{0:T(1024)} %param.13) | copy-start | bytes 1572868
  6.0 0.7 %copy-start.4 = (s32[40,1]{0,1:T(1,128)S(1)}, s32[40,1]{0,1:T(1,128)}, u32[]{:S(2)}) copy-start(s32[40,1]{0,1:T(1,128)} %param.9) | copy-start | bytes 484
  6.7 0.7 %copy-start.5 = (s32[40,1]{0,1:T(1,128)S(1)}, s32[40,1]{0,1:T(1,128)}, u32[]{:S(2)}) copy-start(s32[40,1]{0,1:T(1,128)} %param.10) | copy-start | bytes 484

commit v4 on v3

--- a/solution.py
+++ b/solution.py
@@ -28,11 +28,11 @@
 
 def kernel(
     n_mem, n_camp, plane,
-    gains, costs, rows, cols, count, duals, allowances,
+    gains, costs, rows_in, cols_in, count_in, duals, allowances,
     price, usage, spare,
     g_raw, c_raw, gain, cost, score, run, exp_cost, top_of, weight_of,
     pair, ids, picked, onehot, own_hot, parts, allow,
-    own_id, own_price, own_allow, prev, last,
+    own_id, own_price, own_allow, rows, cols, count, prev, last,
     load_sem, z_send, z_recv, p_send, p_recv, c_send, c_recv,
 ):
     slots, tile = gain.shape[0], gain.shape[1]
@@ -45,7 +45,10 @@
     loads = [
         pltpu.make_async_copy(src, dst, load_sem.at[i])
         for i, (src, dst) in enumerate(
-            ((gains, g_raw), (costs, c_raw), (duals, price), (allowances, allow))
+            (
+                (rows_in, rows), (cols_in, cols), (count_in, count),
+                (duals, price), (allowances, allow), (gains, g_raw), (costs, c_raw),
+            )
         )
     ]
     for load in loads:
@@ -72,6 +75,8 @@
     for peer in peers:
         pl.semaphore_signal(barrier, inc=1, device_id=peer, device_id_type=MESH)
 
+    for load in loads[:3]:
+        load.wait()
     id_rows = ids.shape[1]
     spot = lax.broadcasted_iota(jnp.int32, (id_rows, tile), 0) * tile
     spot = spot + lax.broadcasted_iota(jnp.int32, (id_rows, tile), 1) - me * slots
@@ -125,13 +130,12 @@
             for e in range(1, plane):
                 p_copy(buf, t, d, e).start()
 
-    def gather_wait(buf, t):
-        for d in range(deep):
-            for e in range(1, plane):
-                block = buf.at[owner(d, e)]
-                pltpu.make_async_remote_copy(
-                    block, block, p_send.at[t, d, e], p_recv.at[t, d, e], p_peer(e), MESH
-                ).wait_recv()
+    def gather_wait(buf, t, d):
+        for e in range(1, plane):
+            block = buf.at[owner(d, e)]
+            pltpu.make_async_remote_copy(
+                block, block, p_send.at[t, d, e], p_recv.at[t, d, e], p_peer(e), MESH
+            ).wait_recv()
 
     def gather_drain(buf, t):
         for d in range(1, deep):
@@ -140,8 +144,8 @@
             for e in range(1, plane):
                 p_copy(buf, t, d, e).wait_send()
 
-    loads[2].wait()
     loads[3].wait()
+    loads[4].wait()
 
     def fetch(s, _):
         here = pl.ds(cols[0, s], 1)
@@ -150,8 +154,8 @@
         return 0
 
     lax.fori_loop(0, slots, fetch, 0, unroll=UNROLL)
-    loads[0].wait()
-    loads[1].wait()
+    loads[5].wait()
+    loads[6].wait()
     lane = lax.broadcasted_iota(jnp.int32, (tile, tile), 1)
 
     def camp_copy(t, f):
@@ -269,15 +273,18 @@
         gather_start(picked.at[t], t + 1)
         gather_relay(picked.at[t], t + 1)
         if t == 0:
-            gather_wait(ids, 0)
+            for d in range(deep):
+                gather_wait(ids, 0, d)
             mark()
-        gather_wait(picked.at[t], t + 1)
-
-        rest = picked[t].reshape(n_mem * slots, tile)
-        for i in range(3):
-            part = rest.astype(jnp.bfloat16)
-            parts[:, i * tile : (i + 1) * tile] = part
-            rest = rest - part.astype(jnp.float32)
+        for d in range(deep):
+            gather_wait(picked.at[t], t + 1, d)
+            level = flip(z, d)
+            rest = picked[t, pl.ds(level * plane, plane)].reshape(plane * slots, tile)
+            here = pl.ds(pl.multiple_of(level * (plane * slots), 32), plane * slots)
+            for i in range(3):
+                part = rest.astype(jnp.bfloat16)
+                parts[here, i * tile : (i + 1) * tile] = part
+                rest = rest - part.astype(jnp.float32)
 
         if t < ROUNDS - 1:
             own_price[...] = advance(own_price[...], summed_by(own_hot[...]), own_allow[...])
@@ -312,13 +319,12 @@
     id_rows = -(-n_mem * slots // (8 * tile)) * 8
     f32, bf16 = jnp.float32, jnp.bfloat16
     anywhere = pl.BlockSpec(memory_space=pl.ANY)
-    scalar = pl.BlockSpec(memory_space=pltpu.SMEM)
     dma = pltpu.SemaphoreType.DMA
     shapes = ((blocks, tile), (blocks, tile), (MB, tile))
     held = pl.pallas_call(
         functools.partial(kernel, n_mem, n_camp, plane),
         out_shape=tuple(pltpu.VMEM(shape, f32) for shape in shapes),
-        in_specs=[anywhere, anywhere, scalar, scalar, scalar, anywhere, anywhere],
+        in_specs=[anywhere] * 7,
         out_specs=(pl.BlockSpec(memory_space=pltpu.VMEM),) * 3,
         scratch_shapes=[
             pltpu.VMEM((slots, tile, tile), bf16),
@@ -340,9 +346,12 @@
             pltpu.VMEM((slots, tile), jnp.int32),
             pltpu.VMEM((slots, tile), f32),
             pltpu.VMEM((slots, tile), f32),
+            pltpu.SMEM((1, slots), jnp.int32),
+            pltpu.SMEM((1, slots), jnp.int32),
+            pltpu.SMEM((1, 1), jnp.int32),
             pltpu.SMEM((slots,), jnp.int32),
             pltpu.SMEM((MB,), jnp.int32),
-            dma((4,)),
+            dma((7,)),
             dma((ROUNDS + 1, deep)),
             dma((ROUNDS + 1, deep)),
             dma((ROUNDS + 1, deep, plane)),
@@ -351,7 +360,7 @@
             dma((ROUNDS, n_camp)),
         ],
         compiler_params=pltpu.CompilerParams(
-            collective_id=0, has_side_effects=True, vmem_limit_bytes=44 * 1024 * 1024
+            collective_id=0, has_side_effects=True, vmem_limit_bytes=56 * 1024 * 1024
         ),
     )(
         gains, costs, tile_rows.T, tile_cols.T, tile_count,

time: 52.2 us -> 45.7 us (0.88)
  local copies, waits for them, and re-layouts: 6.02 us -> 0 us
    unnamed x12 -> x0, local copies, waits for them, and re-layouts: 6.02 us -> none
where the time goes in v4:
time: 45.7 us; the launch traced here: 45.6 us
  Pallas kernels  44.3 us (97%)
  between operations  1.29 us (3%)
    pallas_call x1, Pallas kernels, local(): pl.pallas_call(functools.partial(kernel, n_mem, n_camp, plane), out_shape...  43.3 us
    pallas_call x1, Pallas kernels, local(): pl.pallas_call(hand_over, out_shape=tuple((jax.ShapeDtypeStruct(shape, f3...  1 us

profile of v4, /device:TPU:0, one launch (start us, length us, event | category | flops | bytes accessed | tf_op | source)
XLA Modules:
  0.0 45.6 jit_solution(7642190347458773559)
XLA Ops:
  1.3 43.3 %shard_map.94 = (f32[1024,128]{1,0:T(8,128)S(1)}, f32[1024,128]{1,0:T(8,128)S(1)}, f32[8,128]{1,0:T(8,128)S(1)}) custom-call(bf16[40,128,128]{2,1,0:T(8,128)(2,1)} %gains.1, bf16[40,128,128]{2,1,0:T(8,128)(2,1)} %costs.1, s32[1,40]{1,0:T(1,128)} %bitcast.9, s32[1,40]{1,0:T(1,128)} %bitcast.10, s32[1,1]{1,0:T(1,128)S(6)} %copy.10.count_in, ...), custom_call_target="tpu_custom_call" | custom-call | tf_op jit(solution)/shard_map/pallas_call | solution.py:324
  44.6 1.0 %shard_map.95 = (f32[1024,128]{1,0:T(8,128)}, f32[1024,128]{1,0:T(8,128)}, f32[8,128]{1,0:T(8,128)}) custom-call(f32[1024,128]{1,0:T(8,128)S(1)} %get-tuple-element.9.price, f32[1024,128]{1,0:T(8,128)S(1)} %get-tuple-element.10.usage, f32[8,128]{1,0:T(8,128)S(1)} %get-tuple-element.11.spare), custom_call_target="tpu_custom_call" | custom-call | tf_op jit(solution)/shard_map/pallas_call | solution.py:369

commit v5 on v4

--- a/solution.py
+++ b/solution.py
@@ -14,7 +14,7 @@
 STEP_SIZE = 0.2
 SCALE = math.log2(math.e) / SMOOTHING
 MESH = pl.DeviceIdType.MESH
-UNROLL = 8
+UNROLL = 20
 
 
 def flip(i, d):
@@ -230,14 +230,13 @@
             total = jnp.sum(run[last[k]], axis=1, keepdims=True)
             return jnp.where(lane == k + MB, total, packed)
 
-        pair[t, me_c] = lax.fori_loop(0, MB, sums, packed, unroll=MB)
+        packed = lax.fori_loop(0, MB, sums, packed, unroll=MB)
+        pair[t, me_c] = jnp.transpose(packed)[: 2 * MB]
         for f in range(1, n_camp):
             camp_copy(t, f).start()
 
         if t == 0:
             gather_relay(ids, 0)
-        else:
-            dense()
 
         for f in range(1, n_camp):
             block = pair.at[t, lax.rem(me_c - f + n_camp, n_camp)]
@@ -245,19 +244,19 @@
                 block, block, c_send.at[t, f], c_recv.at[t, f], c_peer(f), MESH
             ).wait_recv()
 
-        mine = pair[t, me_c]
-        top = pair[t, 0]
+        mine = pair[t, me_c, :MB]
+        top = pair[t, 0, :MB]
         for c in range(1, n_camp):
-            top = jnp.maximum(top, pair[t, c])
-        denom = jnp.zeros((tile, tile), jnp.float32)
+            top = jnp.maximum(top, pair[t, c, :MB])
+        denom = jnp.zeros((MB, tile), jnp.float32)
         for c in range(n_camp):
-            theirs = pair[t, c]
-            denom = denom + jnp.exp2(theirs - top) * pltpu.roll(theirs, tile - MB, 1)
+            denom = denom + jnp.exp2(pair[t, c, :MB] - top) * pair[t, c, MB:]
         left = jnp.exp2(-top)
         denom = left + denom
         weight = jnp.exp2(mine - top) / denom
         if t == ROUNDS - 1:
-            spare[...] = jnp.transpose(left / denom)[:MB]
+            spare[...] = left / denom
+        weight = jnp.transpose(jnp.concatenate([weight] * (tile // MB), axis=0))
         for k in range(MB):
             weight_of[k] = jnp.broadcast_to(weight[:, k : k + 1], (tile, tile))
 
@@ -276,6 +275,8 @@
             for d in range(deep):
                 gather_wait(ids, 0, d)
             mark()
+        else:
+            dense()
         for d in range(deep):
             gather_wait(picked.at[t], t + 1, d)
             level = flip(z, d)
@@ -336,7 +337,7 @@
             pltpu.VMEM((slots, tile, tile), f32),
             pltpu.VMEM((MB, tile, tile), f32),
             pltpu.VMEM((MB, tile, tile), f32),
-            pltpu.VMEM((ROUNDS, n_camp, tile, tile), f32),
+            pltpu.VMEM((ROUNDS, n_camp, 2 * MB, tile), f32),
             pltpu.VMEM((n_mem, id_rows, tile), jnp.int32),
             pltpu.VMEM((ROUNDS, n_mem, slots, tile), f32),
             pltpu.VMEM((blocks, n_mem * slots), bf16),

time: 45.7 us -> 45.1 us (0.987)
  Pallas kernels: 44.3 us -> 43.7 us
    pallas_call x1, Pallas kernels: 43.3 us -> 42.7 us  [local(): pl.pallas_call(functools.partial(kernel, n_mem, n_camp, plane), out_shape...]
where the time goes in v5:
time: 45.1 us; the launch traced here: 45 us
  Pallas kernels  43.7 us (97%)
  between operations  1.29 us (3%)
    pallas_call x1, Pallas kernels, local(): pl.pallas_call(functools.partial(kernel, n_mem, n_camp, plane), out_shape...  42.7 us
    pallas_call x1, Pallas kernels, local(): pl.pallas_call(hand_over, out_shape=tuple((jax.ShapeDtypeStruct(shape, f3...  1 us

profile of v5, /device:TPU:0, one launch (start us, length us, event | category | flops | bytes accessed | tf_op | source)
XLA Modules:
  0.0 45.0 jit_solution(8335189253963629506)
XLA Ops:
  1.3 42.7 %shard_map.94 = (f32[1024,128]{1,0:T(8,128)S(1)}, f32[1024,128]{1,0:T(8,128)S(1)}, f32[8,128]{1,0:T(8,128)S(1)}) custom-call(bf16[40,128,128]{2,1,0:T(8,128)(2,1)} %gains.1, bf16[40,128,128]{2,1,0:T(8,128)(2,1)} %costs.1, s32[1,40]{1,0:T(1,128)} %bitcast.9, s32[1,40]{1,0:T(1,128)} %bitcast.10, s32[1,1]{1,0:T(1,128)S(6)} %copy.10.count_in, ...), custom_call_target="tpu_custom_call" | custom-call | tf_op jit(solution)/shard_map/pallas_call | solution.py:325
  44.0 1.0 %shard_map.95 = (f32[1024,128]{1,0:T(8,128)}, f32[1024,128]{1,0:T(8,128)}, f32[8,128]{1,0:T(8,128)}) custom-call(f32[1024,128]{1,0:T(8,128)S(1)} %get-tuple-element.9.price, f32[1024,128]{1,0:T(8,128)S(1)} %get-tuple-element.10.usage, f32[8,128]{1,0:T(8,128)S(1)} %get-tuple-element.11.spare), custom_call_target="tpu_custom_call" | custom-call | tf_op jit(solution)/shard_map/pallas_call | solution.py:370

commit v6 on v5

--- a/solution.py
+++ b/solution.py
@@ -54,17 +54,18 @@
     for load in loads:
         load.start()
 
+    level = [flip(z, d) for d in range(deep)]
+    place_of = [flip(b, e) for e in range(plane)]
+    owners = [[row * plane + column for column in place_of] for row in level]
+
     def z_peer(d):
-        return {"mem": flip(z, d) * plane + b, "camp": me_c}
+        return {"mem": owners[d][0], "camp": me_c}
 
     def p_peer(e):
-        return {"mem": z * plane + flip(b, e), "camp": me_c}
+        return {"mem": owners[0][e], "camp": me_c}
 
     def c_peer(f):
         return {"mem": me, "camp": lax.rem(me_c + f, n_camp)}
-
-    def owner(d, e):
-        return flip(z, d) * plane + flip(b, e)
 
     barrier = pltpu.get_barrier_semaphore()
     peers = (
@@ -109,33 +110,46 @@
             buf.at[me], buf.at[me], z_send.at[t, d], z_recv.at[t, d], z_peer(d), MESH
         )
 
-    def p_copy(buf, t, d, e):
-        block = buf.at[owner(d, 0)]
+    def p_copy(buf, t, d, e, column=0, to=None):
+        block = buf.at[owners[d][column]]
         return pltpu.make_async_remote_copy(
-            block, block, p_send.at[t, d, e], p_recv.at[t, d, e], p_peer(e), MESH
+            block, block, p_send.at[t, d, e], p_recv.at[t, d, e], p_peer(to or e), MESH
         )
+
+    def via(d):
+        return 1 + d % 2 if plane == 4 and d < deep - 1 else 0
+
+    def p_start(buf, t, d):
+        for e in range(1, plane):
+            if e < 3 or not via(d):
+                p_copy(buf, t, d, e).start()
+
+    def p_wait(buf, t, d, e):
+        p_copy(buf, t, d, e, column=e).wait_recv()
+
+    def p_forward(buf, t, d):
+        if via(d):
+            p_wait(buf, t, d, 3 - via(d))
+            p_copy(buf, t, d, 3, column=3 - via(d), to=via(d)).start()
 
     def gather_start(buf, t):
         for d in range(1, deep):
             z_copy(buf, t, d).start()
-        for e in range(1, plane):
-            p_copy(buf, t, 0, e).start()
+        p_start(buf, t, 0)
 
     def gather_relay(buf, t):
         for d in range(1, deep):
-            block = buf.at[owner(d, 0)]
+            block = buf.at[owners[d][0]]
             pltpu.make_async_remote_copy(
                 block, block, z_send.at[t, d], z_recv.at[t, d], z_peer(d), MESH
             ).wait_recv()
-            for e in range(1, plane):
-                p_copy(buf, t, d, e).start()
+            p_start(buf, t, d)
+            p_forward(buf, t, d - 1)
 
     def gather_wait(buf, t, d):
         for e in range(1, plane):
-            block = buf.at[owner(d, e)]
-            pltpu.make_async_remote_copy(
-                block, block, p_send.at[t, d, e], p_recv.at[t, d, e], p_peer(e), MESH
-            ).wait_recv()
+            if not (via(d) and e == 3 - via(d)):
+                p_wait(buf, t, d, e)
 
     def gather_drain(buf, t):
         for d in range(1, deep):
@@ -279,9 +293,8 @@
             dense()
         for d in range(deep):
             gather_wait(picked.at[t], t + 1, d)
-            level = flip(z, d)
-            rest = picked[t, pl.ds(level * plane, plane)].reshape(plane * slots, tile)
-            here = pl.ds(pl.multiple_of(level * (plane * slots), 32), plane * slots)
+            rest = picked[t, pl.ds(level[d] * plane, plane)].reshape(plane * slots, tile)
+            here = pl.ds(pl.multiple_of(level[d] * (plane * slots), 32), plane * slots)
             for i in range(3):
                 part = rest.astype(jnp.bfloat16)
                 parts[here, i * tile : (i + 1) * tile] = part

time: 45.1 us -> 50.5 us (1.12)
  Pallas kernels: 43.7 us -> 49 us
    pallas_call x1, Pallas kernels: 42.7 us -> 48 us  [local(): pl.pallas_call(functools.partial(kernel, n_mem, n_camp, plane), out_shape...]
where the time goes in v6:
time: 50.5 us; the launch traced here: 50.3 us
  Pallas kernels  49 us (97%)
  between operations  1.29 us (3%)
    pallas_call x1, Pallas kernels, local(): pl.pallas_call(functools.partial(kernel, n_mem, n_camp, plane), out_shape...  48 us

profile of v6, /device:TPU:0, one launch (start us, length us, event | category | flops | bytes accessed | tf_op | source)
XLA Modules:
  0.0 50.3 jit_solution(17722543854380193654)
XLA Ops:
  1.3 48.0 %shard_map.94 = (f32[1024,128]{1,0:T(8,128)S(1)}, f32[1024,128]{1,0:T(8,128)S(1)}, f32[8,128]{1,0:T(8,128)S(1)}) custom-call(bf16[40,128,128]{2,1,0:T(8,128)(2,1)} %gains.1, bf16[40,128,128]{2,1,0:T(8,128)(2,1)} %costs.1, s32[1,40]{1,0:T(1,128)} %bitcast.9, s32[1,40]{1,0:T(1,128)} %bitcast.10, s32[1,1]{1,0:T(1,128)S(6)} %copy.10.count_in, ...), custom_call_target="tpu_custom_call" | custom-call | tf_op jit(solution)/shard_map/pallas_call | solution.py:338
  49.3 1.0 %shard_map.95 = (f32[1024,128]{1,0:T(8,128)}, f32[1024,128]{1,0:T(8,128)}, f32[8,128]{1,0:T(8,128)}) custom-call(f32[1024,128]{1,0:T(8,128)S(1)} %get-tuple-element.9.price, f32[1024,128]{1,0:T(8,128)S(1)} %get-tuple-element.10.usage, f32[8,128]{1,0:T(8,128)S(1)} %get-tuple-element.11.spare), custom_call_target="tpu_custom_call" | custom-call | tf_op jit(solution)/shard_map/pallas_call | solution.py:383

commit v7 on v6

--- a/solution.py
+++ b/solution.py
@@ -54,6 +54,7 @@
     for load in loads:
         load.start()
 
+    direct = range(1, min(2, deep))
     level = [flip(z, d) for d in range(deep)]
     place_of = [flip(b, e) for e in range(plane)]
     owners = [[row * plane + column for column in place_of] for row in level]
@@ -63,6 +64,9 @@
 
     def p_peer(e):
         return {"mem": owners[0][e], "camp": me_c}
+
+    def d_peer(d, e):
+        return {"mem": owners[d][e], "camp": me_c}
 
     def c_peer(f):
         return {"mem": me, "camp": lax.rem(me_c + f, n_camp)}
@@ -71,6 +75,7 @@
     peers = (
         [z_peer(d) for d in range(1, deep)]
         + [p_peer(e) for e in range(1, plane)]
+        + [d_peer(d, e) for d in direct for e in range(1, plane)]
         + [c_peer(f) for f in range(1, n_camp)]
     )
     for peer in peers:
@@ -110,53 +115,45 @@
             buf.at[me], buf.at[me], z_send.at[t, d], z_recv.at[t, d], z_peer(d), MESH
         )
 
-    def p_copy(buf, t, d, e, column=0, to=None):
-        block = buf.at[owners[d][column]]
+    def p_copy(buf, t, d, e, block, peer):
+        block = buf.at[block]
         return pltpu.make_async_remote_copy(
-            block, block, p_send.at[t, d, e], p_recv.at[t, d, e], p_peer(to or e), MESH
+            block, block, p_send.at[t, d, e], p_recv.at[t, d, e], peer, MESH
         )
 
-    def via(d):
-        return 1 + d % 2 if plane == 4 and d < deep - 1 else 0
-
-    def p_start(buf, t, d):
+    def z_wait(buf, t, d):
+        block = buf.at[owners[d][0]]
+        pltpu.make_async_remote_copy(
+            block, block, z_send.at[t, d], z_recv.at[t, d], z_peer(d), MESH
+        ).wait_recv()
+
+    def gather_start(buf, t):
+        for d in reversed(range(1, deep)):
+            z_copy(buf, t, d).start()
         for e in range(1, plane):
-            if e < 3 or not via(d):
-                p_copy(buf, t, d, e).start()
-
-    def p_wait(buf, t, d, e):
-        p_copy(buf, t, d, e, column=e).wait_recv()
-
-    def p_forward(buf, t, d):
-        if via(d):
-            p_wait(buf, t, d, 3 - via(d))
-            p_copy(buf, t, d, 3, column=3 - via(d), to=via(d)).start()
-
-    def gather_start(buf, t):
-        for d in range(1, deep):
-            z_copy(buf, t, d).start()
-        p_start(buf, t, 0)
+            p_copy(buf, t, 0, e, me, p_peer(e)).start()
+        for d in direct:
+            for e in range(1, plane):
+                p_copy(buf, t, d, e, me, d_peer(d, e)).start()
 
     def gather_relay(buf, t):
-        for d in range(1, deep):
-            block = buf.at[owners[d][0]]
-            pltpu.make_async_remote_copy(
-                block, block, z_send.at[t, d], z_recv.at[t, d], z_peer(d), MESH
-            ).wait_recv()
-            p_start(buf, t, d)
-            p_forward(buf, t, d - 1)
+        for d in range(len(direct) + 1, deep):
+            z_wait(buf, t, d)
+            for e in range(1, plane):
+                p_copy(buf, t, d, e, owners[d][0], p_peer(e)).start()
 
     def gather_wait(buf, t, d):
+        if d in direct:
+            z_wait(buf, t, d)
         for e in range(1, plane):
-            if not (via(d) and e == 3 - via(d)):
-                p_wait(buf, t, d, e)
+            p_copy(buf, t, d, e, owners[d][e], p_peer(e)).wait_recv()
 
     def gather_drain(buf, t):
         for d in range(1, deep):
             z_copy(buf, t, d).wait_send()
         for d in range(deep):
             for e in range(1, plane):
-                p_copy(buf, t, d, e).wait_send()
+                p_copy(buf, t, d, e, me, p_peer(e)).wait_send()
 
     loads[3].wait()
     loads[4].wait()

time: 50.5 us -> 44.3 us (0.88)
  Pallas kernels: 49 us -> 42.8 us
    pallas_call x1, Pallas kernels: 48 us -> 41.9 us  [local(): pl.pallas_call(functools.partial(kernel, n_mem, n_camp, plane), out_shape...]
where the time goes in v7:
time: 44.3 us; the launch traced here: 44.1 us
  Pallas kernels  42.8 us (97%)
  between operations  1.29 us (3%)
    pallas_call x1, Pallas kernels, local(): pl.pallas_call(functools.partial(kernel, n_mem, n_camp, plane), out_shape...  41.9 us
    pallas_call x1, Pallas kernels, local(): pl.pallas_call(hand_over, out_shape=tuple((jax.ShapeDtypeStruct(shape, f3...  1 us

profile of v7, /device:TPU:0, one launch (start us, length us, event | category | flops | bytes accessed | tf_op | source)
XLA Modules:
  0.0 44.1 jit_solution(10443494558050389994)
XLA Ops:
  1.3 41.9 %shard_map.94 = (f32[1024,128]{1,0:T(8,128)S(1)}, f32[1024,128]{1,0:T(8,128)S(1)}, f32[8,128]{1,0:T(8,128)S(1)}) custom-call(bf16[40,128,128]{2,1,0:T(8,128)(2,1)} %gains.1, bf16[40,128,128]{2,1,0:T(8,128)(2,1)} %costs.1, s32[1,40]{1,0:T(1,128)} %bitcast.9, s32[1,40]{1,0:T(1,128)} %bitcast.10, s32[1,1]{1,0:T(1,128)S(6)} %copy.10.count_in, ...), custom_call_target="tpu_custom_call" | custom-call | tf_op jit(solution)/shard_map/pallas_call | solution.py:335
  43.1 1.0 %shard_map.95 = (f32[1024,128]{1,0:T(8,128)}, f32[1024,128]{1,0:T(8,128)}, f32[8,128]{1,0:T(8,128)}) custom-call(f32[1024,128]{1,0:T(8,128)S(1)} %get-tuple-element.9.price, f32[1024,128]{1,0:T(8,128)S(1)} %get-tuple-element.10.usage, f32[8,128]{1,0:T(8,128)S(1)} %get-tuple-element.11.spare), custom_call_target="tpu_custom_call" | custom-call | tf_op jit(solution)/shard_map/pallas_call | solution.py:380

commit v8 on v7

--- a/solution.py
+++ b/solution.py
@@ -54,7 +54,7 @@
     for load in loads:
         load.start()
 
-    direct = range(1, min(2, deep))
+    direct = range(1, min(3, deep))
     level = [flip(z, d) for d in range(deep)]
     place_of = [flip(b, e) for e in range(plane)]
     owners = [[row * plane + column for column in place_of] for row in level]

time: 44.3 us -> 43.8 us (0.989)
    pallas_call x1, Pallas kernels: 41.9 us -> 41.4 us  [local(): pl.pallas_call(functools.partial(kernel, n_mem, n_camp, plane), out_shape...]
where the time goes in v8:
time: 43.8 us; the launch traced here: 43.6 us
  Pallas kernels  42.4 us (97%)
  between operations  1.29 us (3%)
    pallas_call x1, Pallas kernels, local(): pl.pallas_call(functools.partial(kernel, n_mem, n_camp, plane), out_shape...  41.4 us
    pallas_call x1, Pallas kernels, local(): pl.pallas_call(hand_over, out_shape=tuple((jax.ShapeDtypeStruct(shape, f3...  1 us

profile of v8, /device:TPU:0, one launch (start us, length us, event | category | flops | bytes accessed | tf_op | source)
XLA Modules:
  0.0 43.6 jit_solution(13724067003135254983)
XLA Ops:
  1.3 41.4 %shard_map.94 = (f32[1024,128]{1,0:T(8,128)S(1)}, f32[1024,128]{1,0:T(8,128)S(1)}, f32[8,128]{1,0:T(8,128)S(1)}) custom-call(bf16[40,128,128]{2,1,0:T(8,128)(2,1)} %gains.1, bf16[40,128,128]{2,1,0:T(8,128)(2,1)} %costs.1, s32[1,40]{1,0:T(1,128)} %bitcast.9, s32[1,40]{1,0:T(1,128)} %bitcast.10, s32[1,1]{1,0:T(1,128)S(6)} %copy.10.count_in, ...), custom_call_target="tpu_custom_call" | custom-call | tf_op jit(solution)/shard_map/pallas_call | solution.py:335
  42.6 1.0 %shard_map.95 = (f32[1024,128]{1,0:T(8,128)}, f32[1024,128]{1,0:T(8,128)}, f32[8,128]{1,0:T(8,128)}) custom-call(f32[1024,128]{1,0:T(8,128)S(1)} %get-tuple-element.9.price, f32[1024,128]{1,0:T(8,128)S(1)} %get-tuple-element.10.usage, f32[8,128]{1,0:T(8,128)S(1)} %get-tuple-element.11.spare), custom_call_target="tpu_custom_call" | custom-call | tf_op jit(solution)/shard_map/pallas_call | solution.py:380
